TPU v7x, 512 devices: a whole 4x4x16 slice. The times are simulated.
512 devices in a mesh: dp: 512 (over y, x, z, core).
Axes of the slice: x: 4, y: 4, z: 16, core: 2. Of those that a mesh axis runs over, the one named last changes fastest.
Arguments:
- picture_encoder_result: float32 [131072, 1152], P('dp'), may hold values from -0.1875 to 0.1875
- caption_encoder_result: float32 [131072, 1152], P('dp'), may hold values from -0.1875 to 0.1875
- picture_channel_factor: float32 [1152], replicated, may hold values from 0.25 to 1.75
- caption_channel_factor: float32 [1152], replicated, may hold values from 0.25 to 1.75
- logit_multiplier: float32 [], replicated, may hold values from 5 to 15
- logit_offset: float32 [], replicated, may hold values from -4 to -1
Outputs:
- image_grad: float32 [131072, 1152], P('dp')
- text_grad: float32 [131072, 1152], P('dp')
- image_gain_grad: float32 [1152], replicated
- text_gain_grad: float32 [1152], replicated
- temp_grad: float32 [], replicated
- bias_grad: float32 [], replicated
- loss: float32 [], replicated
All inputs are finite; a program needn't handle non-finite values.
Results may differ from a plain program's by a relative error of at most 0.00012.
Values sent between devices are 32-bit elements; how exact they have to be, the bound alone decides.
A program may use at most 64 MiB of HBM per device.

v0:
```python
import jax
import jax.numpy as jnp
from jax import lax
from jax.sharding import PartitionSpec as P

eps = 1e-06


def swapped(shard, axis, stride):
    return lax.ppermute(shard, axis, [(i, i ^ 1 << stride) for i in range(lax.axis_size(axis))])


def normalize(feat, gain):
    scaled = feat * gain
    norm = jnp.sqrt(jnp.sum(scaled * scaled, axis=-1, keepdims=True) + eps)
    return (scaled / norm, norm)


def partner_round_loop(
    picture_unit_rows, caption_unit_rows, logit_multiplier, logit_offset, resident_slice
):
    round_update = jnp.dot(
        picture_unit_rows,
        caption_unit_rows.T,
        precision=lax.Precision.HIGHEST,
        preferred_element_type=jnp.float32,
    )
    match_logit_matrix = logit_multiplier * round_update + logit_offset
    labels = resident_slice * jnp.eye(picture_unit_rows.shape[0], dtype=jnp.float32)
    pair_loss = jnp.sum(jax.nn.softplus(match_logit_matrix) - labels * match_logit_matrix)
    derivative_collection = jax.nn.sigmoid(match_logit_matrix) - labels
    picture_vector_derivative = logit_multiplier * jnp.dot(
        derivative_collection,
        caption_unit_rows,
        precision=lax.Precision.HIGHEST,
        preferred_element_type=jnp.float32,
    )
    caption_vector_derivative = logit_multiplier * jnp.dot(
        derivative_collection.T,
        picture_unit_rows,
        precision=lax.Precision.HIGHEST,
        preferred_element_type=jnp.float32,
    )
    return (
        picture_vector_derivative,
        caption_vector_derivative,
        pair_loss,
        jnp.sum(derivative_collection * round_update),
        jnp.sum(derivative_collection),
    )


def backward_norm(d_emb, emb, norm, feat, gain):
    d_scaled = (d_emb - emb * jnp.sum(emb * d_emb, axis=-1, keepdims=True)) / norm
    return (d_scaled * gain, jnp.sum(d_scaled * feat, axis=0))


def shards(
    picture_encoder_result,
    caption_encoder_result,
    picture_channel_factor,
    caption_channel_factor,
    logit_multiplier,
    logit_offset,
):
    picture_unit_rows, image_norm = normalize(picture_encoder_result, picture_channel_factor)
    caption_unit_rows, text_norm = normalize(caption_encoder_result, caption_channel_factor)
    log_dev = lax.axis_size("dp").bit_length() - 1
    far = log_dev - 1
    near = log_dev // 2
    bit_list = [far, near]
    picture_vector_derivative, caption_vector_derivative, loss_sum, temp_sum, bias_sum = (
        partner_round_loop(
            picture_unit_rows, caption_unit_rows, logit_multiplier, logit_offset, 1.0
        )
    )
    for bit in bit_list:
        partner_caption_slice = swapped(caption_unit_rows, "dp", bit)
        d_img, d_txt, losses, temps, biases = partner_round_loop(
            picture_unit_rows, partner_caption_slice, logit_multiplier, logit_offset, 0.0
        )
        caption_vector_derivative = caption_vector_derivative + swapped(d_txt, "dp", bit)
        picture_vector_derivative = picture_vector_derivative + d_img
        loss_sum = loss_sum + losses
        temp_sum = temp_sum + temps
        bias_sum = bias_sum + biases
    image_grad, image_gain_part = backward_norm(
        picture_vector_derivative,
        picture_unit_rows,
        image_norm,
        picture_encoder_result,
        picture_channel_factor,
    )
    text_grad, text_gain_part = backward_norm(
        caption_vector_derivative,
        caption_unit_rows,
        text_norm,
        caption_encoder_result,
        caption_channel_factor,
    )
    image_gain_grad, text_gain_grad, temp_total, bias_total, loss_total = lax.psum(
        (image_gain_part, text_gain_part, temp_sum, bias_sum, loss_sum), "dp"
    )
    pair_count = (
        3.0
        * picture_encoder_result.shape[0]
        * picture_encoder_result.shape[0]
        * lax.axis_size("dp")
    )
    return (
        image_grad,
        text_grad,
        image_gain_grad,
        text_gain_grad,
        temp_total / pair_count,
        bias_total / pair_count,
        loss_total / pair_count,
    )


def solution(mesh):
    return jax.shard_map(
        shards,
        mesh=mesh,
        in_specs=(P("dp", None), P("dp", None), P(), P(), P(), P()),
        out_specs=(P("dp", None), P("dp", None), P(), P(), P(), P(), P()),
        check_vma=False,
    )
```

profile of v0, /device:TPU:1, one launch (start us, length us, event | category | flops | bytes accessed | tf_op | source)
XLA Modules:
  0.0 344.7 jit_solution(5072679024662920535)
XLA Ops:
  0.7 1.6 multiply_reduce_fusion.4
  2.2 0.0 copy-done
  2.3 0.0 copy-done.3
  2.3 0.2 multiply_divide_fusion
  2.5 0.4 copy-done.5
  2.8 16.3 %collective-permute-start.1 = (f32[256,1152]{1,0:T(8,128)S(1)}, f32[256,1152]{1,0:T(8,128)}, u32[]{:S(2)}, u32[]{:S(2)}) collective-permute-start(f32[256,1152]{1,0:T(8,128)S(1)} %multiply_divide_fusion), channel_id=1, source_target_pairs={{0,16},{1,17},{2,18},{3,19},{4,20},{5,21},{6,22},{7,23},{8,24},{9,... | collective-permute-start | bytes 3538952 | tf_op jit(solution)/shard_map/ppermute | solution.py:10
  19.1 4.8 %collective-permute-start = (f32[256,1152]{1,0:T(8,128)S(1)}, f32[256,1152]{1,0:T(8,128)}, u32[]{:S(2)}, u32[]{:S(2)}) collective-permute-start(f32[256,1152]{1,0:T(8,128)S(1)} %multiply_divide_fusion), channel_id=1, source_target_pairs={{0,256},{1,257},{2,258},{3,259},{4,260},{5,261},{6,262},{7,263},{8... | collective-permute-start | bytes 3538952 | tf_op jit(solution)/shard_map/ppermute | solution.py:10
  24.0 0.2 multiply_reduce_fusion.5
  24.2 0.6 add_sqrt_fusion.1
  26.0 0.0 copy-start.8
  26.0 3.0 fusion.4
  29.1 28.3 %collective-permute-done.1 = f32[256,1152]{1,0:T(8,128)} collective-permute-done((f32[256,1152]{1,0:T(8,128)S(1)}, f32[256,1152]{1,0:T(8,128)}, u32[]{:S(2)}, u32[]{:S(2)}) %collective-permute-start.1) | collective-permute-done | bytes 1179680 | tf_op jit(solution)/shard_map/ppermute | solution.py:10
  57.4 3.4 fusion.8
  60.8 2.4 convolution_multiply_fusion
  63.2 18.0 %collective-permute-start.3 = (f32[256,1152]{1,0:T(8,128)}, f32[256,1152]{1,0:T(8,128)}, u32[]{:S(2)}, u32[]{:S(2)}) collective-permute-start(f32[256,1152]{1,0:T(8,128)} %convolution_multiply_fusion), channel_id=1, source_target_pairs={{0,16},{1,17},{2,18},{3,19},{4,20},{5,21},{6,22},{7,23},{8,24},{9,... | collective-permute-start | bytes 3538952 | tf_op jit(solution)/shard_map/ppermute | solution.py:10
  81.3 0.0 collective-permute-done
  81.3 3.5 %fusion.6 = (f32[]{:T(128)}, f32[]{:T(128)}, f32[]{:T(128)}, f32[256,256]{1,0:T(8,128)S(1)}) fusion(f32[]{:T(128)S(6)} %copy.14, f32[]{:T(128)S(6)} %copy.13, f32[256,1152]{1,0:T(8,128)} %collective-permute-done, f32[256,1152]{1,0:T(8,128)S(1)} %copy-done.1, f32[256]{0:T(256)S(1)} %copy-done.8, f32[1152]{0:T(1024)S(1)} %copy-done.4), kind=kOutput, calls=%fused_computation.26 | convolution fusion | flops 907673600 | bytes 2627092 | tf_op jit(solution)/shard_map/dot_general | solution.py:22
  84.8 2.4 convolution_multiply_fusion.1
  87.2 0.0 copy-done.2
  87.2 5.0 %collective-permute-start.2 = (f32[256,1152]{1,0:T(8,128)}, f32[256,1152]{1,0:T(8,128)}, u32[]{:S(2)}, u32[]{:S(2)}) collective-permute-start(f32[256,1152]{1,0:T(8,128)} %convolution_multiply_fusion.1), channel_id=1, source_target_pairs={{0,256},{1,257},{2,258},{3,259},{4,260},{5,261},{6,262},{7,263},{8... | collective-permute-start | bytes 3538952 | tf_op jit(solution)/shard_map/ppermute | solution.py:10
  92.2 0.0 copy-done.12
  92.2 0.0 copy-done.6
  92.2 1.4 fusion.12
  99.3 0.0 copy-start.9
  99.3 2.7 convolution_add_fusion.1
  102.0 2.8 multiply_reduce_fusion.3
  104.9 1.4 multiply_reduce_fusion.1
  106.3 46.1 %collective-permute-done.3 = f32[256,1152]{1,0:T(8,128)} collective-permute-done((f32[256,1152]{1,0:T(8,128)}, f32[256,1152]{1,0:T(8,128)}, u32[]{:S(2)}, u32[]{:S(2)}) %collective-permute-start.3) | collective-permute-done | bytes 1179680 | tf_op jit(solution)/shard_map/ppermute | solution.py:10
  152.4 0.0 collective-permute-done.2
  152.4 3.3 multiply_reduce_fusion.2
  155.7 1.4 multiply_reduce_fusion
  157.1 182.2 %all-reduce = (f32[1152]{0:T(1024)}, f32[1152]{0:T(1024)}, f32[]{:T(128)}, f32[]{:T(128)}, f32[]{:T(128)}) all-reduce(f32[1152]{0:T(1024)S(1)} %get-tuple-element.23, f32[1152]{0:T(1024)S(1)} %get-tuple-element.21, f32[]{:T(128)S(6)} %add.103, f32[]{:T(128)S(6)} %add.105, f32[]{:T(128)S(6)} %add.110), channel_id=1, replica_groups=mesh['dp'=512] {'dp'}, use_global_device_ids=true, to_apply=%region_5.6 | all-reduce | flops 2307 | bytes 18456 | tf_op jit(solution)/shard_map/psum | solution.py:101
  (21 shorter events, 0.0 us)
Async XLA Ops:
  0.6 1.6 copy-start
  0.6 1.6 copy-start.3
  2.3 0.6 copy-start.5
  2.3 21.7 %copy-start.1 = (f32[256,1152]{1,0:T(8,128)S(1)}, f32[256,1152]{1,0:T(8,128)}, u32[]{:S(2)}) copy-start(f32[256,1152]{1,0:T(8,128)} %param.6) | copy-start | bytes 3538948
  2.3 21.7 %copy-start.4 = (f32[1152]{0:T(1024)S(1)}, f32[1152]{0:T(1024)}, u32[]{:S(2)}) copy-start(f32[1152]{0:T(1024)} %param.8) | copy-start | bytes 13828
  2.8 54.6 %collective-permute-start.1 = (f32[256,1152]{1,0:T(8,128)S(1)}, f32[256,1152]{1,0:T(8,128)}, u32[]{:S(2)}, u32[]{:S(2)}) collective-permute-start(f32[256,1152]{1,0:T(8,128)S(1)} %multiply_divide_fusion), channel_id=1, source_target_pairs={{0,16},{1,17},{2,18},{3,19},{4,20},{5,21},{6,22},{7,23},{8,24},{9,... | collective-permute-start | bytes 3538952 | tf_op jit(solution)/shard_map/ppermute | solution.py:10
  19.1 62.2 %collective-permute-start = (f32[256,1152]{1,0:T(8,128)S(1)}, f32[256,1152]{1,0:T(8,128)}, u32[]{:S(2)}, u32[]{:S(2)}) collective-permute-start(f32[256,1152]{1,0:T(8,128)S(1)} %multiply_divide_fusion), channel_id=1, source_target_pairs={{0,256},{1,257},{2,258},{3,259},{4,260},{5,261},{6,262},{7,263},{8... | collective-permute-start | bytes 3538952 | tf_op jit(solution)/shard_map/ppermute | solution.py:10
  26.0 31.4 %copy-start.8 = (f32[256]{0:T(256)S(1)}, f32[256]{0:T(256)}, u32[]{:S(2)}) copy-start(f32[256]{0:T(256)} %add_sqrt_fusion.1) | copy-start | bytes 3076
  29.1 63.2 %copy-start.12 = (f32[256,256]{1,0:T(8,128)}, f32[256,256]{1,0:T(8,128)S(1)}, u32[]{:S(2)}) copy-start(f32[256,256]{1,0:T(8,128)S(1)} %get-tuple-element.29) | copy-start | bytes 786436
  60.8 2.4 copy-start.10
  63.2 89.2 %collective-permute-start.3 = (f32[256,1152]{1,0:T(8,128)}, f32[256,1152]{1,0:T(8,128)}, u32[]{:S(2)}, u32[]{:S(2)}) collective-permute-start(f32[256,1152]{1,0:T(8,128)} %convolution_multiply_fusion), channel_id=1, source_target_pairs={{0,16},{1,17},{2,18},{3,19},{4,20},{5,21},{6,22},{7,23},{8,24},{9,... | collective-permute-start | bytes 3538952 | tf_op jit(solution)/shard_map/ppermute | solution.py:10
  84.8 2.4 copy-start.2
  84.8 7.5 %copy-start.6 = (f32[256]{0:T(256)S(1)}, f32[256]{0:T(256)}, u32[]{:S(2)}) copy-start(f32[256]{0:T(256)} %copy-done.5) | copy-start | bytes 3076
  87.2 65.2 %collective-permute-start.2 = (f32[256,1152]{1,0:T(8,128)}, f32[256,1152]{1,0:T(8,128)}, u32[]{:S(2)}, u32[]{:S(2)}) collective-permute-start(f32[256,1152]{1,0:T(8,128)} %convolution_multiply_fusion.1), channel_id=1, source_target_pairs={{0,256},{1,257},{2,258},{3,259},{4,260},{5,261},{6,262},{7,263},{8... | collective-permute-start | bytes 3538952 | tf_op jit(solution)/shard_map/ppermute | solution.py:10
  99.3 2.7 copy-start.9
  99.3 2.7 copy-start.11
  104.9 47.5 %copy-start.7 = (f32[256]{0:T(256)S(1)}, f32[256]{0:T(256)}, u32[]{:S(2)}) copy-start(f32[256]{0:T(256)} %copy-done.5) | copy-start | bytes 3076
  104.9 47.5 %copy-start.13 = (f32[256,256]{1,0:T(8,128)S(1)}, f32[256,256]{1,0:T(8,128)}, u32[]{:S(2)}) copy-start(f32[256,256]{1,0:T(8,128)} %copy-done.12) | copy-start | bytes 786436
where the time goes:
time: 345 us
  blocking collectives  182 us (53%)
  waiting for transfers between devices  74.4 us (22%)
  starting transfers between devices  44.1 us (13%)
  matrix products  25 us (7%)
  between operations  13.1 us (4%)
  other arithmetic  5.35 us (2%)
    psum x1, blocking collectives, shards(): lax.psum((image_gain_part, text_gain_part, temp_sum, bias_sum, loss_sum),...  182 us
    ppermute x4, waiting for transfers between devices, swapped(): lax.ppermute(shard, axis, [(i, i ^ 1 << stride) for i in range(lax.axis_s...  74.4 us
    ppermute x4, starting transfers between devices, swapped(): lax.ppermute(shard, axis, [(i, i ^ 1 << stride) for i in range(lax.axis_s...  44.1 us
    dot_general x3, matrix products, partner_round_loop(): jnp.dot(picture_unit_rows, caption_unit_rows.T, precision=lax.Precision.H...  9.89 us
    dot_general x3, matrix products, partner_round_loop(): jnp.dot(derivative_collection.T, picture_unit_rows, precision=lax.Precisi...  8.14 us
    dot_general x3, matrix products, partner_round_loop(): jnp.dot(derivative_collection, caption_unit_rows, precision=lax.Precision...  6.96 us
  transfers between devices with their start and end apart: 4, of which 2 were waited for; matrix products, arithmetic and copies ran while one was open for 7% of the time, Pallas kernels for 0%

commit v1 on v0

v1 whole, which is shorter than its diff:
```python
import functools

import jax
import jax.numpy as jnp
from jax import lax
from jax.experimental import pallas as pl
from jax.experimental.pallas import tpu as pltpu
from jax.sharding import PartitionSpec as P

eps = 1e-06
MESH = pl.DeviceIdType.MESH

ROWS = 256
D = 1152
CHUNKS = 2
CHUNK = ROWS // CHUNKS
HALF = CHUNK // 2
Z = 16
HOPS = Z // 2
BITS = 9
FAR_BIT = 8
NEAR_BIT = 4
SUM_BITS = (0, 5, 6, 7, 8, 1, 2, 3, 4)
LANES = 128
TILES = D // LANES
PAY = 24
SELF, FAR, NEAR = 0, 1, 2


def flipped(me, bit):
    stride = 1 << bit
    return me + stride - 2 * stride * ((me // stride) % 2)


def z_shifted(me, step):
    z = (me // 2) % Z
    return me + 2 * ((z + step + Z) % Z - z)


def matmul(a, b, contract):
    return lax.dot_general(
        a,
        b,
        ((contract[:1], contract[1:]), ((), ())),
        precision=lax.Precision.HIGHEST,
        preferred_element_type=jnp.float32,
    )


def kernel(
    mult_ref,
    offs_ref,
    img_hbm,
    txt_hbm,
    gi_ref,
    gt_ref,
    img_grad_ref,
    txt_grad_ref,
    img_gain_ref,
    txt_gain_ref,
    sums_ref,
    img_raw,
    txt_raw,
    img_emb,
    d_img,
    hops,
    ret,
    far_in,
    far_ret,
    far_back,
    g_all,
    e_all,
    gain_acc,
    sum_acc,
    pay,
    pay_in,
    load_sem,
    send_sem,
    recv_sem,
    far_send,
    far_recv,
    pay_send,
    pay_recv,
):
    me = lax.axis_index("dp")
    ways = (z_shifted(me, 1), z_shifted(me, -1))
    far = flipped(me, FAR_BIT)
    mult = mult_ref[0]
    offs = offs_ref[0]

    barrier = pltpu.get_barrier_semaphore()
    for other in ways + tuple(flipped(me, bit) for bit in range(BITS)):
        pl.semaphore_signal(barrier, inc=1, device_id=(other,), device_id_type=MESH)
    pl.semaphore_wait(barrier, BITS + 2)

    def hop(phase, h, k, d, src):
        return pltpu.make_async_remote_copy(
            src_ref=src,
            dst_ref=hops.at[phase, h, k, pl.ds(d * HALF, HALF)],
            send_sem=send_sem.at[phase, h, k, d],
            recv_sem=recv_sem.at[phase, h, k, d],
            device_id=(ways[d],),
            device_id_type=MESH,
        )

    def landed(phase, h, k, d):
        return hops.at[phase, h, k, pl.ds(d * HALF, HALF)]

    def forward(phase, h, k):
        for d in range(2):
            src = landed(phase, h, k, d)
            hop(phase, h, k, d, src).wait_recv()
            hop(phase, h + 1, k, d, src).start()

    def sent(phase, h, k):
        for d in range(2):
            hop(phase, h, k, d, landed(phase, h, k, d)).wait_send()

    def far_copy(leg, k, src, dst):
        return pltpu.make_async_remote_copy(
            src_ref=src.at[pl.ds(k * CHUNK, CHUNK)],
            dst_ref=dst.at[pl.ds(k * CHUNK, CHUNK)],
            send_sem=far_send.at[leg, k],
            recv_sem=far_recv.at[leg, k],
            device_id=(far,),
            device_id_type=MESH,
        )

    def pay_copy(step):
        return pltpu.make_async_remote_copy(
            src_ref=pay.at[step],
            dst_ref=pay_in.at[step],
            send_sem=pay_send.at[step],
            recv_sem=pay_recv.at[step],
            device_id=(flipped(me, SUM_BITS[step]),),
            device_id_type=MESH,
        )

    def block(src, dst, pair, k):
        rows = pl.ds(k * CHUNK, CHUNK)
        feat = src[...]
        gain = gt_ref[...]
        scaled = feat * gain
        norm = jnp.sqrt(jnp.sum(scaled * scaled, axis=-1, keepdims=True) + eps)
        emb = scaled / norm
        e_all[pair, rows] = emb
        image = img_emb[...]
        dots = matmul(emb, image, (1, 1))
        logits = mult * dots + offs
        small = jnp.exp(-jnp.abs(logits))
        loss = jnp.maximum(logits, 0.0) + jnp.log1p(small)
        g = jnp.where(logits >= 0.0, 1.0, small) / (1.0 + small)
        if pair == SELF:
            text_row = k * CHUNK + lax.broadcasted_iota(jnp.int32, (CHUNK, ROWS), 0)
            image_row = lax.broadcasted_iota(jnp.int32, (CHUNK, ROWS), 1)
            labels = (text_row == image_row).astype(jnp.float32)
            loss = loss - labels * logits
            g = g - labels
        g_all[pair, rows] = g
        for i, term in enumerate((loss, g * dots, g)):
            line = jnp.sum(term, axis=0, keepdims=True)
            sum_acc[i : i + 1] += line[:, :LANES] + line[:, LANES:]
        d_emb = mult * matmul(g, image, (1, 0))
        d_scaled = (d_emb - emb * jnp.sum(emb * d_emb, axis=-1, keepdims=True)) / norm
        dst[...] = d_scaled * gain
        gain_acc[...] += jnp.sum(d_scaled * feat, axis=0, keepdims=True)

    def image_side(pair):
        for half in range(2):
            cols = pl.ds(half * CHUNK, CHUNK)
            part = mult * matmul(g_all[pair, :, cols], e_all[pair], (0, 0))
            if pair == SELF:
                d_img[cols] = part
            else:
                d_img[cols] += part

    def image_norm():
        for half in range(2):
            rows = pl.ds(half * CHUNK, CHUNK)
            scaled = img_raw[rows] * gi_ref[...]
            norm = jnp.sqrt(jnp.sum(scaled * scaled, axis=-1, keepdims=True) + eps)
            img_emb[rows] = scaled / norm

    def image_finish():
        total = jnp.zeros((1, D), jnp.float32)
        for half in range(2):
            rows = pl.ds(half * CHUNK, CHUNK)
            feat = img_raw[rows]
            gain = gi_ref[...]
            scaled = feat * gain
            norm = jnp.sqrt(jnp.sum(scaled * scaled, axis=-1, keepdims=True) + eps)
            emb = img_emb[rows]
            d_emb = d_img[rows]
            d_scaled = (
                d_emb - emb * jnp.sum(emb * d_emb, axis=-1, keepdims=True)
            ) / norm
            img_grad_ref[rows] = d_scaled * gain
            total = total + jnp.sum(d_scaled * feat, axis=0, keepdims=True)
        text = gain_acc[...]
        pay[0] = jnp.zeros((PAY, LANES), jnp.float32)
        for i in range(TILES):
            pay[0, i : i + 1] = total[:, i * LANES : (i + 1) * LANES]
            pay[0, TILES + i : TILES + i + 1] = text[:, i * LANES : (i + 1) * LANES]
        pay[0, 2 * TILES : 2 * TILES + 3] = sum_acc[0:3]

    def sum_step(step):
        pay_copy(step).wait_recv()
        pay[step + 1] = pay[step] + pay_in[step]

    def sum_finish():
        total = pay[BITS]
        for i in range(TILES):
            cols = pl.ds(i * LANES, LANES)
            img_gain_ref[:, cols] = total[i : i + 1]
            txt_gain_ref[:, cols] = total[TILES + i : TILES + i + 1]
        for i in range(3):
            line = total[2 * TILES + i : 2 * TILES + i + 1]
            sums_ref[i] = jnp.sum(line) / (3.0 * ROWS * ROWS * (1 << BITS))

    def self_block(k):
        rows = pl.ds(k * CHUNK, CHUNK)
        block(txt_raw.at[rows], txt_grad_ref.at[rows], SELF, k)

    def far_block(k):
        rows = pl.ds(k * CHUNK, CHUNK)
        far_copy(0, k, txt_hbm, far_in).wait_recv()
        block(far_in.at[rows], far_ret.at[rows], FAR, k)
        far_copy(1, k, far_ret, far_back).start()

    def far_add(k):
        rows = pl.ds(k * CHUNK, CHUNK)
        far_copy(1, k, far_ret, far_back).wait_recv()
        txt_grad_ref[rows] += far_back[rows]

    for k in range(CHUNKS):
        for d in range(2):
            hop(0, 0, k, d, txt_hbm.at[pl.ds(k * CHUNK + d * HALF, HALF)]).start()
    for k in range(CHUNKS):
        far_copy(0, k, txt_hbm, far_in).start()
    loads = [
        pltpu.make_async_copy(img_hbm, img_raw, load_sem.at[0]),
        pltpu.make_async_copy(txt_hbm, txt_raw, load_sem.at[1]),
    ]
    for load in loads:
        load.start()
    gain_acc[...] = jnp.zeros_like(gain_acc)
    sum_acc[...] = jnp.zeros_like(sum_acc)
    for load in loads:
        load.wait()
    image_norm()

    work = {
        0: lambda: self_block(0),
        1: lambda: self_block(1),
        2: lambda: image_side(SELF),
        5: lambda: far_block(0),
        6: lambda: far_block(1),
        7: lambda: image_side(FAR),
        12: lambda: far_add(0),
        13: lambda: far_add(1),
    }
    for h in range(HOPS - 1):
        for k in range(CHUNKS):
            forward(0, h, k)
            work.get(h * CHUNKS + k, lambda: None)()

    for k in range(CHUNKS):
        for d in range(2):
            hop(0, HOPS - 1, k, d, landed(0, HOPS - 1, k, d)).wait_recv()
        block(hops.at[0, HOPS - 1, k], ret.at[k], NEAR, k)
        for d in range(2):
            hop(1, 0, k, d, ret.at[k, pl.ds(d * HALF, HALF)]).start()

    image_side(NEAR)
    image_finish()
    pay_copy(0).start()
    for h in range(HOPS - 1):
        for k in range(CHUNKS):
            forward(1, h, k)
            step = h * CHUNKS + k - 1
            if 0 <= step < BITS:
                sum_step(step)
                if step + 1 < BITS:
                    pay_copy(step + 1).start()
            if step == BITS:
                sum_finish()
            sent(0, h, k)

    for k in range(CHUNKS):
        for d in range(2):
            hop(1, HOPS - 1, k, d, landed(1, HOPS - 1, k, d)).wait_recv()
        rows = pl.ds(k * CHUNK, CHUNK)
        txt_grad_ref[rows] += hops[1, HOPS - 1, k]

    for k in range(CHUNKS):
        sent(0, HOPS - 1, k)
        for h in range(HOPS):
            sent(1, h, k)
        far_copy(0, k, txt_hbm, far_in).wait_send()
        far_copy(1, k, far_ret, far_back).wait_send()
    for step in range(BITS):
        pay_copy(step).wait_send()


def shards(
    picture_encoder_result,
    caption_encoder_result,
    picture_channel_factor,
    caption_channel_factor,
    logit_multiplier,
    logit_offset,
):
    f32 = jnp.float32
    vmem = pl.BlockSpec(memory_space=pltpu.VMEM)
    smem = pl.BlockSpec(memory_space=pltpu.SMEM)
    hbm = pl.BlockSpec(memory_space=pl.ANY)
    dma = pltpu.SemaphoreType.DMA
    image_grad, text_grad, image_gain, text_gain, sums = pl.pallas_call(
        kernel,
        name="contrast",
        out_shape=(
            jax.ShapeDtypeStruct((ROWS, D), f32),
            jax.ShapeDtypeStruct((ROWS, D), f32),
            jax.ShapeDtypeStruct((1, D), f32),
            jax.ShapeDtypeStruct((1, D), f32),
            jax.ShapeDtypeStruct((3,), f32),
        ),
        in_specs=[smem, smem, hbm, hbm, vmem, vmem],
        out_specs=(vmem, vmem, vmem, vmem, smem),
        scratch_shapes=[
            pltpu.VMEM((ROWS, D), f32),
            pltpu.VMEM((ROWS, D), f32),
            pltpu.VMEM((ROWS, D), f32),
            pltpu.VMEM((ROWS, D), f32),
            pltpu.VMEM((2, HOPS, CHUNKS, CHUNK, D), f32),
            pltpu.VMEM((CHUNKS, CHUNK, D), f32),
            pltpu.VMEM((ROWS, D), f32),
            pltpu.VMEM((ROWS, D), f32),
            pltpu.VMEM((ROWS, D), f32),
            pltpu.VMEM((3, ROWS, ROWS), f32),
            pltpu.VMEM((3, ROWS, D), f32),
            pltpu.VMEM((1, D), f32),
            pltpu.VMEM((8, LANES), f32),
            pltpu.VMEM((BITS + 1, PAY, LANES), f32),
            pltpu.VMEM((BITS, PAY, LANES), f32),
            dma((2,)),
            dma((2, HOPS, CHUNKS, 2)),
            dma((2, HOPS, CHUNKS, 2)),
            dma((2, CHUNKS)),
            dma((2, CHUNKS)),
            dma((BITS,)),
            dma((BITS,)),
        ],
        compiler_params=pltpu.CompilerParams(
            collective_id=0, has_side_effects=True, vmem_limit_bytes=52 << 20
        ),
        cost_estimate=pl.CostEstimate(
            flops=18 * ROWS * ROWS * D,
            bytes_accessed=16 * ROWS * D,
            transcendentals=6 * ROWS * ROWS,
        ),
    )(
        logit_multiplier.reshape(1),
        logit_offset.reshape(1),
        picture_encoder_result,
        caption_encoder_result,
        picture_channel_factor.reshape(1, D),
        caption_channel_factor.reshape(1, D),
    )
    return (
        image_grad,
        text_grad,
        image_gain.reshape(D),
        text_gain.reshape(D),
        sums[1],
        sums[2],
        sums[0],
    )


def solution(mesh):
    return jax.shard_map(
        shards,
        mesh=mesh,
        in_specs=(P("dp", None), P("dp", None), P(), P(), P(), P()),
        out_specs=(P("dp", None), P("dp", None), P(), P(), P(), P(), P()),
        check_vma=False,
    )
```

time: 345 us -> 231 us (0.67)
  Pallas kernels: 0 us -> 223 us
  blocking collectives: 182 us -> 0 us
  waiting for transfers between devices: 74.4 us -> 0 us
  starting transfers between devices: 44.1 us -> 0 us
  matrix products: 25 us -> 0 us
  between operations: 13.1 us -> 1.94 us
  local copies, waits for them, and re-layouts: 0.46 us -> 4.69 us
  other arithmetic: 5.35 us -> 1.24 us
    pallas_call x0 -> x1, Pallas kernels: none -> 223 us  [shards(): pl.pallas_call(kernel, name='contrast', out_shape=(jax.ShapeDtypeStruct((...]
    psum x1 -> x0, blocking collectives: 182 us -> none  [shards(): lax.psum((image_gain_part, text_gain_part, temp_sum, bias_sum, loss_sum),...]
    ppermute x4 -> x0, waiting for transfers between devices: 74.4 us -> none  [swapped(): lax.ppermute(shard, axis, [(i, i ^ 1 << stride) for i in range(lax.axis_s...]
    ppermute x4 -> x0, starting transfers between devices: 44.1 us -> none  [swapped(): lax.ppermute(shard, axis, [(i, i ^ 1 << stride) for i in range(lax.axis_s...]
    dot_general x9 -> x0, matrix products: 25 us -> none  [the longest x3 9.89 us: partner_round_loop(): jnp.dot(picture_unit_rows, caption_unit_rows.T, precision=lax.Precision.H...]
    reduce_sum x4 -> x0, other arithmetic: 4.58 us -> none  [the longest x2 2.82 us: backward_norm(): return (d_scaled * gain, jnp.sum(d_scaled * feat, axis=0))]
  transfers between devices with their start and end apart: 4 -> 0, of which waited for: 2 -> 0; matrix products, arithmetic and copies ran while one was open for 7% -> 0% of each run, Pallas kernels for 0% -> 0%
where the time goes in v1:
time: 231 us
  Pallas kernels  223 us (97%)
  local copies, waits for them, and re-layouts  4.69 us (2%)
    pallas_call x1, Pallas kernels, shards(): pl.pallas_call(kernel, name='contrast', out_shape=(jax.ShapeDtypeStruct((...  223 us

profile of v1, /device:TPU:1, one launch (start us, length us, event | category | flops | bytes accessed | tf_op | source)
XLA Modules:
  0.0 230.7 jit_solution(10532609318104092222)
XLA Ops:
  1.9 0.7 reshape.34.gi_ref
  2.6 0.7 reshape.35.gt_ref
  3.3 222.8 %contrast.1 = (f32[256,1152]{1,0:T(8,128)S(1)}, f32[256,1152]{1,0:T(8,128)}, f32[1,1152]{1,0:T(1,128)S(1)}, f32[1,1152]{1,0:T(1,128)S(1)}, f32[3]{0:T(128)S(1)}) custom-call(f32[1]{0:T(128)} %bitcast.5.mult_ref, f32[1]{0:T(128)} %bitcast.6.offs_ref, f32[256,1152]{1,0:T(8,128)} %img_hbm.1, f32[256,1152]{1,0:T(8,128)} %txt_hbm.1, ...), custom_call_target="tpu_custom_call" | custom-call | flops 1358954496 | bytes 4718592 | tf_op jit(solution)/shard_map/contrast/pallas_call | solution.py:318
  226.2 0.6 reduce
  226.8 0.6 reduce.1
  227.4 0.6 fusion
  228.0 0.0 copy-start
  228.0 1.0 copy.17
  229.0 0.7 copy-done
  229.7 1.0 copy.18
Async XLA Ops:
  228.0 1.7 copy-start

commit v2 on v1

--- a/solution.py
+++ b/solution.py
@@ -20,10 +20,13 @@
 BITS = 9
 FAR_BIT = 8
 NEAR_BIT = 4
-SUM_BITS = (0, 5, 6, 7, 8, 1, 2, 3, 4)
+CROSS_BITS = (2, 3, 4, 5, 6, 7, 8)
+SUM_BITS = (1, 2, 3, 4, 5, 6, 7, 8)
+SUM_SLOTS = (0, 1, 2, 3, 4, 5, 7, 9, 11, 12)
+FAR_SLOTS = (10, 13)
 LANES = 128
 TILES = D // LANES
-PAY = 24
+PAY = TILES + 2
 SELF, FAR, NEAR = 0, 1, 2
 
 
@@ -48,17 +51,19 @@
 
 
 def kernel(
+    mult_hbm,
+    offs_hbm,
+    img_hbm,
+    txt_hbm,
+    gi_hbm,
+    gt_hbm,
+    img_grad_ref,
+    txt_grad_ref,
+    total_ref,
     mult_ref,
     offs_ref,
-    img_hbm,
-    txt_hbm,
     gi_ref,
     gt_ref,
-    img_grad_ref,
-    txt_grad_ref,
-    img_gain_ref,
-    txt_gain_ref,
-    sums_ref,
     img_raw,
     txt_raw,
     img_emb,
@@ -72,8 +77,10 @@
     e_all,
     gain_acc,
     sum_acc,
+    pay_all,
     pay,
     pay_in,
+    ready,
     load_sem,
     send_sem,
     recv_sem,
@@ -83,15 +90,39 @@
     pay_recv,
 ):
     me = lax.axis_index("dp")
+    core = me % 2
+    mate = flipped(me, 0)
     ways = (z_shifted(me, 1), z_shifted(me, -1))
     far = flipped(me, FAR_BIT)
-    mult = mult_ref[0]
-    offs = offs_ref[0]
+
+    def greet(sem, other):
+        pl.semaphore_signal(sem, inc=1, device_id=(other,), device_id_type=MESH)
 
     barrier = pltpu.get_barrier_semaphore()
-    for other in ways + tuple(flipped(me, bit) for bit in range(BITS)):
-        pl.semaphore_signal(barrier, inc=1, device_id=(other,), device_id_type=MESH)
-    pl.semaphore_wait(barrier, BITS + 2)
+    for other in ways:
+        greet(barrier, other - core)
+    for bit in CROSS_BITS:
+        greet(barrier, flipped(me, bit) - core + 1)
+
+    @pl.when(core == 1)
+    def _():
+        greet(barrier, mate)
+        pl.semaphore_wait(ready, 1)
+
+    @pl.when(core == 0)
+    def _():
+        pl.semaphore_wait(barrier, 5)
+        greet(ready, mate)
+
+    def meet_others():
+        @pl.when(core == 1)
+        def _():
+            pl.semaphore_wait(barrier, 2 * len(CROSS_BITS))
+            greet(ready, mate)
+
+        @pl.when(core == 0)
+        def _():
+            pl.semaphore_wait(ready, 1)
 
     def hop(phase, h, k, d, src):
         return pltpu.make_async_remote_copy(
@@ -127,19 +158,20 @@
         )
 
     def pay_copy(step):
+        first, last = step == 0, step == len(SUM_BITS) + 1
         return pltpu.make_async_remote_copy(
-            src_ref=pay.at[step],
-            dst_ref=pay_in.at[step],
+            src_ref=pay_all.at[1 - core] if first else pay.at[step - 1],
+            dst_ref=total_ref.at[core] if last else pay_in.at[step],
             send_sem=pay_send.at[step],
             recv_sem=pay_recv.at[step],
-            device_id=(flipped(me, SUM_BITS[step]),),
+            device_id=(mate if first or last else flipped(me, SUM_BITS[step - 1]),),
             device_id_type=MESH,
         )
 
     def block(src, dst, pair, k):
         rows = pl.ds(k * CHUNK, CHUNK)
         feat = src[...]
-        gain = gt_ref[...]
+        gain = gt_ref[...].reshape(1, D)
         scaled = feat * gain
         norm = jnp.sqrt(jnp.sum(scaled * scaled, axis=-1, keepdims=True) + eps)
         emb = scaled / norm
@@ -177,7 +209,7 @@
     def image_norm():
         for half in range(2):
             rows = pl.ds(half * CHUNK, CHUNK)
-            scaled = img_raw[rows] * gi_ref[...]
+            scaled = img_raw[rows] * gi_ref[...].reshape(1, D)
             norm = jnp.sqrt(jnp.sum(scaled * scaled, axis=-1, keepdims=True) + eps)
             img_emb[rows] = scaled / norm
 
@@ -186,7 +218,7 @@
         for half in range(2):
             rows = pl.ds(half * CHUNK, CHUNK)
             feat = img_raw[rows]
-            gain = gi_ref[...]
+            gain = gi_ref[...].reshape(1, D)
             scaled = feat * gain
             norm = jnp.sqrt(jnp.sum(scaled * scaled, axis=-1, keepdims=True) + eps)
             emb = img_emb[rows]
@@ -197,25 +229,25 @@
             img_grad_ref[rows] = d_scaled * gain
             total = total + jnp.sum(d_scaled * feat, axis=0, keepdims=True)
         text = gain_acc[...]
-        pay[0] = jnp.zeros((PAY, LANES), jnp.float32)
         for i in range(TILES):
-            pay[0, i : i + 1] = total[:, i * LANES : (i + 1) * LANES]
-            pay[0, TILES + i : TILES + i + 1] = text[:, i * LANES : (i + 1) * LANES]
-        pay[0, 2 * TILES : 2 * TILES + 3] = sum_acc[0:3]
+            pay_all[0, i] = total[:, i * LANES : (i + 1) * LANES]
+            pay_all[1, i] = text[:, i * LANES : (i + 1) * LANES]
+        pay_all[0, TILES] = sum_acc[0:1]
+        pay_all[0, TILES + 1] = sum_acc[1:2]
+        pay_all[1, TILES] = sum_acc[2:3]
+        pay_all[1, TILES + 1] = jnp.zeros((1, LANES), jnp.float32)
 
     def sum_step(step):
+        last = len(SUM_BITS) + 1
         pay_copy(step).wait_recv()
-        pay[step + 1] = pay[step] + pay_in[step]
-
-    def sum_finish():
-        total = pay[BITS]
-        for i in range(TILES):
-            cols = pl.ds(i * LANES, LANES)
-            img_gain_ref[:, cols] = total[i : i + 1]
-            txt_gain_ref[:, cols] = total[TILES + i : TILES + i + 1]
-        for i in range(3):
-            line = total[2 * TILES + i : 2 * TILES + i + 1]
-            sums_ref[i] = jnp.sum(line) / (3.0 * ROWS * ROWS * (1 << BITS))
+        if step == 0:
+            pay[0] = pay_all[core] + pay_in[0]
+        elif step < last:
+            pay[step] = pay[step - 1] + pay_in[step]
+        if step == last - 1:
+            total_ref[core] = pay[step]
+        if step < last:
+            pay_copy(step + 1).start()
 
     def self_block(k):
         rows = pl.ds(k * CHUNK, CHUNK)
@@ -235,11 +267,18 @@
     for k in range(CHUNKS):
         for d in range(2):
             hop(0, 0, k, d, txt_hbm.at[pl.ds(k * CHUNK + d * HALF, HALF)]).start()
-    for k in range(CHUNKS):
-        far_copy(0, k, txt_hbm, far_in).start()
     loads = [
-        pltpu.make_async_copy(img_hbm, img_raw, load_sem.at[0]),
-        pltpu.make_async_copy(txt_hbm, txt_raw, load_sem.at[1]),
+        pltpu.make_async_copy(src, dst, load_sem.at[i])
+        for i, (src, dst) in enumerate(
+            (
+                (mult_hbm, mult_ref),
+                (offs_hbm, offs_ref),
+                (gi_hbm, gi_ref),
+                (gt_hbm, gt_ref),
+                (img_hbm, img_raw),
+                (txt_hbm, txt_raw),
+            )
+        )
     ]
     for load in loads:
         load.start()
@@ -247,17 +286,23 @@
     sum_acc[...] = jnp.zeros_like(sum_acc)
     for load in loads:
         load.wait()
+    mult = mult_ref[0]
+    offs = offs_ref[0]
     image_norm()
+
+    def far_start():
+        meet_others()
+        for k in range(CHUNKS):
+            far_copy(0, k, txt_hbm, far_in).start()
 
     work = {
         0: lambda: self_block(0),
         1: lambda: self_block(1),
-        2: lambda: image_side(SELF),
-        5: lambda: far_block(0),
-        6: lambda: far_block(1),
-        7: lambda: image_side(FAR),
-        12: lambda: far_add(0),
-        13: lambda: far_add(1),
+        2: far_start,
+        3: lambda: image_side(SELF),
+        9: lambda: far_block(0),
+        10: lambda: far_block(1),
+        11: lambda: image_side(FAR),
     }
     for h in range(HOPS - 1):
         for k in range(CHUNKS):
@@ -277,13 +322,11 @@
     for h in range(HOPS - 1):
         for k in range(CHUNKS):
             forward(1, h, k)
-            step = h * CHUNKS + k - 1
-            if 0 <= step < BITS:
-                sum_step(step)
-                if step + 1 < BITS:
-                    pay_copy(step + 1).start()
-            if step == BITS:
-                sum_finish()
+            slot = h * CHUNKS + k
+            if slot in SUM_SLOTS:
+                sum_step(SUM_SLOTS.index(slot))
+            if slot in FAR_SLOTS:
+                far_add(FAR_SLOTS.index(slot))
             sent(0, h, k)
 
     for k in range(CHUNKS):
@@ -298,8 +341,32 @@
             sent(1, h, k)
         far_copy(0, k, txt_hbm, far_in).wait_send()
         far_copy(1, k, far_ret, far_back).wait_send()
-    for step in range(BITS):
+    for step in range(len(SUM_SLOTS)):
         pay_copy(step).wait_send()
+
+
+def finish(
+    img_ref, txt_ref, total_ref, img_out, txt_out, gi_out, gt_out, *rest
+):
+    sums_out, sems = rest[:3], rest[3]
+    copies = [
+        pltpu.make_async_copy(img_ref, img_out, sems.at[0]),
+        pltpu.make_async_copy(txt_ref, txt_out, sems.at[1]),
+    ]
+    for copy in copies:
+        copy.start()
+    for i in range(TILES):
+        cols = pl.ds(i * LANES, LANES)
+        gi_out[cols] = total_ref[0, i, 0]
+        gt_out[cols] = total_ref[1, i, 0]
+    for out, line in zip(
+        sums_out, (total_ref[0, TILES + 1], total_ref[1, TILES], total_ref[0, TILES])
+    ):
+        out[...] = jnp.sum(line, axis=-1, keepdims=True) / (
+            3.0 * ROWS * ROWS * (1 << BITS)
+        )
+    for copy in copies:
+        copy.wait()
 
 
 def shards(
@@ -312,22 +379,24 @@
 ):
     f32 = jnp.float32
     vmem = pl.BlockSpec(memory_space=pltpu.VMEM)
-    smem = pl.BlockSpec(memory_space=pltpu.SMEM)
-    hbm = pl.BlockSpec(memory_space=pl.ANY)
+    hbm = pl.BlockSpec(memory_space=pltpu.HBM)
     dma = pltpu.SemaphoreType.DMA
-    image_grad, text_grad, image_gain, text_gain, sums = pl.pallas_call(
+    wide = jax.ShapeDtypeStruct((ROWS, D), f32)
+    image_grad, text_grad, total = pl.pallas_call(
         kernel,
         name="contrast",
         out_shape=(
-            jax.ShapeDtypeStruct((ROWS, D), f32),
-            jax.ShapeDtypeStruct((ROWS, D), f32),
-            jax.ShapeDtypeStruct((1, D), f32),
-            jax.ShapeDtypeStruct((1, D), f32),
-            jax.ShapeDtypeStruct((3,), f32),
+            wide,
+            wide,
+            jax.ShapeDtypeStruct((2, PAY, 1, LANES), f32),
         ),
-        in_specs=[smem, smem, hbm, hbm, vmem, vmem],
-        out_specs=(vmem, vmem, vmem, vmem, smem),
+        in_specs=[hbm] * 6,
+        out_specs=(vmem, vmem, vmem),
         scratch_shapes=[
+            pltpu.SMEM((1,), f32),
+            pltpu.SMEM((1,), f32),
+            pltpu.VMEM((D,), f32),
+            pltpu.VMEM((D,), f32),
             pltpu.VMEM((ROWS, D), f32),
             pltpu.VMEM((ROWS, D), f32),
             pltpu.VMEM((ROWS, D), f32),
@@ -341,18 +410,20 @@
             pltpu.VMEM((3, ROWS, D), f32),
             pltpu.VMEM((1, D), f32),
             pltpu.VMEM((8, LANES), f32),
-            pltpu.VMEM((BITS + 1, PAY, LANES), f32),
-            pltpu.VMEM((BITS, PAY, LANES), f32),
-            dma((2,)),
+            pltpu.VMEM((2, PAY, 1, LANES), f32),
+            pltpu.VMEM((len(SUM_SLOTS) - 1, PAY, 1, LANES), f32),
+            pltpu.VMEM((len(SUM_SLOTS) - 1, PAY, 1, LANES), f32),
+            pltpu.SemaphoreType.REGULAR,
+            dma((6,)),
             dma((2, HOPS, CHUNKS, 2)),
             dma((2, HOPS, CHUNKS, 2)),
             dma((2, CHUNKS)),
             dma((2, CHUNKS)),
-            dma((BITS,)),
-            dma((BITS,)),
+            dma((len(SUM_SLOTS),)),
+            dma((len(SUM_SLOTS),)),
         ],
         compiler_params=pltpu.CompilerParams(
-            collective_id=0, has_side_effects=True, vmem_limit_bytes=52 << 20
+            collective_id=0, has_side_effects=True, vmem_limit_bytes=51 << 20
         ),
         cost_estimate=pl.CostEstimate(
             flops=18 * ROWS * ROWS * D,
@@ -364,18 +435,21 @@
         logit_offset.reshape(1),
         picture_encoder_result,
         caption_encoder_result,
-        picture_channel_factor.reshape(1, D),
-        caption_channel_factor.reshape(1, D),
+        pltpu.with_memory_space_constraint(picture_channel_factor, pltpu.HBM),
+        pltpu.with_memory_space_constraint(caption_channel_factor, pltpu.HBM),
     )
-    return (
-        image_grad,
-        text_grad,
-        image_gain.reshape(D),
-        text_gain.reshape(D),
-        sums[1],
-        sums[2],
-        sums[0],
-    )
+    one = jax.ShapeDtypeStruct((1, 1), f32)
+    line = jax.ShapeDtypeStruct((D,), f32)
+    *results, temp, bias, loss = pl.pallas_call(
+        finish,
+        name="results",
+        out_shape=(wide, wide, line, line, one, one, one),
+        in_specs=[vmem] * 3,
+        out_specs=(hbm, hbm, vmem, vmem, vmem, vmem, vmem),
+        scratch_shapes=[dma((2,))],
+        compiler_params=pltpu.CompilerParams(vmem_limit_bytes=8 << 20),
+    )(image_grad, text_grad, total)
+    return (*results, temp[0, 0], bias[0, 0], loss[0, 0])
 
 
 def solution(mesh):

time: 231 us -> 222 us (0.961)
  local copies, waits for them, and re-layouts: 4.69 us -> 0 us
  Pallas kernels: 223 us -> 220 us
    pallas_call x1 -> x2, Pallas kernels: 223 us -> 220 us  [the longest x1 218 us: shards(): pl.pallas_call(kernel, name='contrast', out_shape=(wide, wide, jax.ShapeD...]
    unnamed x4 -> x0, local copies, waits for them, and re-layouts: 2.71 us -> none
where the time goes in v2:
time: 222 us
  Pallas kernels  220 us (99%)
    pallas_call x1, Pallas kernels, shards(): pl.pallas_call(kernel, name='contrast', out_shape=(wide, wide, jax.ShapeD...  218 us

profile of v2, /device:TPU:1, one launch (start us, length us, event | category | flops | bytes accessed | tf_op | source)
XLA Modules:
  0.0 221.8 jit_solution(13087233664705035276)
XLA Ops:
  1.9 217.7 %contrast.1 = (f32[256,1152]{1,0:T(8,128)S(1)}, f32[256,1152]{1,0:T(8,128)S(1)}, f32[2,11,1,128]{3,2,1,0:T(1,128)S(1)}) custom-call(f32[1]{0:T(128)} %bitcast.5.mult_hbm, f32[1]{0:T(128)} %bitcast.6.offs_hbm, f32[256,1152]{1,0:T(8,128)} %img_hbm.1, f32[256,1152]{1,0:T(8,128)} %txt_hbm.1, f32[1152]{0:T(1024)} %gi_hbm.1, f32[1152]{0:T(1024)} %gt_hbm.1), custom_call_target="tpu_custom_call" | custom-call | flops 1358954496 | bytes 4718592 | tf_op jit(solution)/shard_map/contrast/pallas_call | solution.py:385
  219.6 2.0 results.1

commit v3 on v2

--- a/solution.py
+++ b/solution.py
@@ -20,10 +20,11 @@
 BITS = 9
 FAR_BIT = 8
 NEAR_BIT = 4
-CROSS_BITS = (2, 3, 4, 5, 6, 7, 8)
-SUM_BITS = (1, 2, 3, 4, 5, 6, 7, 8)
-SUM_SLOTS = (0, 1, 2, 3, 4, 5, 7, 9, 11, 12)
-FAR_SLOTS = (10, 13)
+CROSS_BITS = (5, 6, 7, 8)
+SUM_BITS = (0, 1, 2, 3, 4, 5, 6, 7, 8, 4, 0)
+ACROSS = len(SUM_BITS) - 2
+SUM_SLOTS = (2, 3, 4, 5, 7, 8, 9, 10, 11, 13, 14)
+FAR_SLOTS = (8, 12)
 LANES = 128
 TILES = D // LANES
 PAY = TILES + 2
@@ -81,6 +82,8 @@
     pay,
     pay_in,
     ready,
+    quarter,
+    far_in_kernel,
     load_sem,
     send_sem,
     recv_sem,
@@ -98,18 +101,29 @@
     def greet(sem, other):
         pl.semaphore_signal(sem, inc=1, device_id=(other,), device_id_type=MESH)
 
+    place = (me // 2) % Z
+    lower = place < HOPS
+    upper = place >= HOPS
     barrier = pltpu.get_barrier_semaphore()
     for other in ways:
-        greet(barrier, other - core)
-    for bit in CROSS_BITS:
-        greet(barrier, flipped(me, bit) - core + 1)
-
-    @pl.when(core == 1)
+        greet(barrier, other - core * (1 - (other // 2) % Z // HOPS))
+
+    @pl.when(upper)
+    def _():
+        greet(barrier, mate)
+        pl.semaphore_wait(barrier, 3)
+
+    @pl.when(lower)
+    def _():
+        for bit in CROSS_BITS:
+            greet(barrier, flipped(me, bit) - core + 1)
+
+    @pl.when(lower & (core == 1))
     def _():
         greet(barrier, mate)
         pl.semaphore_wait(ready, 1)
 
-    @pl.when(core == 0)
+    @pl.when(lower & (core == 0))
     def _():
         pl.semaphore_wait(barrier, 5)
         greet(ready, mate)
@@ -123,6 +137,23 @@
         @pl.when(core == 0)
         def _():
             pl.semaphore_wait(ready, 1)
+
+    def at_ends(act):
+        @pl.when(place == 0)
+        def _():
+            act(-1)
+
+        @pl.when(place == HOPS - 1)
+        def _():
+            act(1)
+
+    def quarter_in(_):
+        greet(quarter, far)
+
+    def tell_quarter(way):
+        pl.semaphore_wait(quarter, 1)
+        for i in range(1, HOPS // 2 + 1):
+            greet(far_in_kernel, z_shifted(me, way * i))
 
     def hop(phase, h, k, d, src):
         return pltpu.make_async_remote_copy(
@@ -158,15 +189,27 @@
         )
 
     def pay_copy(step):
-        first, last = step == 0, step == len(SUM_BITS) + 1
+        first, last = step == 0, step == len(SUM_BITS) - 1
         return pltpu.make_async_remote_copy(
             src_ref=pay_all.at[1 - core] if first else pay.at[step - 1],
             dst_ref=total_ref.at[core] if last else pay_in.at[step],
             send_sem=pay_send.at[step],
             recv_sem=pay_recv.at[step],
-            device_id=(mate if first or last else flipped(me, SUM_BITS[step - 1]),),
+            device_id=(flipped(me, SUM_BITS[step]),),
             device_id_type=MESH,
         )
+
+    def on_senders(step, act):
+        if step <= 4 or step > ACROSS:
+            act()
+        else:
+            pl.when(lower)(act)
+
+    def on_receivers(step, act):
+        if step == ACROSS:
+            pl.when(upper)(act)
+        else:
+            on_senders(step, act)
 
     def block(src, dst, pair, k):
         rows = pl.ds(k * CHUNK, CHUNK)
@@ -238,16 +281,27 @@
         pay_all[1, TILES + 1] = jnp.zeros((1, LANES), jnp.float32)
 
     def sum_step(step):
-        last = len(SUM_BITS) + 1
-        pay_copy(step).wait_recv()
-        if step == 0:
-            pay[0] = pay_all[core] + pay_in[0]
-        elif step < last:
-            pay[step] = pay[step - 1] + pay_in[step]
-        if step == last - 1:
+        last = len(SUM_BITS) - 1
+
+        def take():
+            pay_copy(step).wait_recv()
+            if step == 0:
+                pay[0] = pay_all[core] + pay_in[0]
+            elif step < ACROSS:
+                pay[step] = pay[step - 1] + pay_in[step]
+            elif step == ACROSS:
+                pay[step] = pay_in[step]
+
+        on_receivers(step, take)
+        if step == ACROSS:
+
+            @pl.when(lower)
+            def _():
+                pay[step] = pay[step - 1]
+
             total_ref[core] = pay[step]
         if step < last:
-            pay_copy(step + 1).start()
+            on_senders(step + 1, lambda: pay_copy(step + 1).start())
 
     def self_block(k):
         rows = pl.ds(k * CHUNK, CHUNK)
@@ -291,18 +345,29 @@
     image_norm()
 
     def far_start():
-        meet_others()
         for k in range(CHUNKS):
             far_copy(0, k, txt_hbm, far_in).start()
+
+    def lower_start():
+        @pl.when(lower)
+        def _():
+            meet_others()
+            far_start()
+
+    def upper_start():
+        @pl.when(upper)
+        def _():
+            pl.semaphore_wait(far_in_kernel, 1)
+            far_start()
 
     work = {
         0: lambda: self_block(0),
         1: lambda: self_block(1),
-        2: far_start,
+        2: lower_start,
         3: lambda: image_side(SELF),
-        9: lambda: far_block(0),
-        10: lambda: far_block(1),
-        11: lambda: image_side(FAR),
+        HOPS - 1: lambda: at_ends(quarter_in),
+        HOPS: lambda: at_ends(tell_quarter),
+        HOPS + 2: upper_start,
     }
     for h in range(HOPS - 1):
         for k in range(CHUNKS):
@@ -316,13 +381,22 @@
         for d in range(2):
             hop(1, 0, k, d, ret.at[k, pl.ds(d * HALF, HALF)]).start()
 
+    def add_up():
+        far_block(1)
+        image_side(FAR)
+        image_finish()
+        pay_copy(0).start()
+
+    work = {
+        0: lambda: far_block(0),
+        1: add_up,
+    }
     image_side(NEAR)
-    image_finish()
-    pay_copy(0).start()
     for h in range(HOPS - 1):
         for k in range(CHUNKS):
             forward(1, h, k)
             slot = h * CHUNKS + k
+            work.get(slot, lambda: None)()
             if slot in SUM_SLOTS:
                 sum_step(SUM_SLOTS.index(slot))
             if slot in FAR_SLOTS:
@@ -334,6 +408,9 @@
             hop(1, HOPS - 1, k, d, landed(1, HOPS - 1, k, d)).wait_recv()
         rows = pl.ds(k * CHUNK, CHUNK)
         txt_grad_ref[rows] += hops[1, HOPS - 1, k]
+        slot = (HOPS - 1) * CHUNKS + k
+        if slot in SUM_SLOTS:
+            sum_step(SUM_SLOTS.index(slot))
 
     for k in range(CHUNKS):
         sent(0, HOPS - 1, k)
@@ -341,8 +418,8 @@
             sent(1, h, k)
         far_copy(0, k, txt_hbm, far_in).wait_send()
         far_copy(1, k, far_ret, far_back).wait_send()
-    for step in range(len(SUM_SLOTS)):
-        pay_copy(step).wait_send()
+    for step in range(len(SUM_BITS)):
+        on_senders(step, lambda: pay_copy(step).wait_send())
 
 
 def finish(
@@ -413,6 +490,8 @@
             pltpu.VMEM((2, PAY, 1, LANES), f32),
             pltpu.VMEM((len(SUM_SLOTS) - 1, PAY, 1, LANES), f32),
             pltpu.VMEM((len(SUM_SLOTS) - 1, PAY, 1, LANES), f32),
+            pltpu.SemaphoreType.REGULAR,
+            pltpu.SemaphoreType.REGULAR,
             pltpu.SemaphoreType.REGULAR,
             dma((6,)),
             dma((2, HOPS, CHUNKS, 2)),

time: 222 us -> 222 us (level)
  no operation moved by 1% of the time
where the time goes in v3:
time: 222 us
  Pallas kernels  220 us (99%)
    pallas_call x1, Pallas kernels, shards(): pl.pallas_call(kernel, name='contrast', out_shape=(wide, wide, jax.ShapeD...  217 us

profile of v3, /device:TPU:1, one launch (start us, length us, event | category | flops | bytes accessed | tf_op | source)
XLA Modules:
  0.0 221.6 jit_solution(7018707760057980547)
XLA Ops:
  1.9 217.5 %contrast.1 = (f32[256,1152]{1,0:T(8,128)S(1)}, f32[256,1152]{1,0:T(8,128)S(1)}, f32[2,11,1,128]{3,2,1,0:T(1,128)S(1)}) custom-call(f32[1]{0:T(128)} %bitcast.5.mult_hbm, f32[1]{0:T(128)} %bitcast.6.offs_hbm, f32[256,1152]{1,0:T(8,128)} %img_hbm.1, f32[256,1152]{1,0:T(8,128)} %txt_hbm.1, f32[1152]{0:T(1024)} %gi_hbm.1, f32[1152]{0:T(1024)} %gt_hbm.1), custom_call_target="tpu_custom_call" | custom-call | flops 1358954496 | bytes 4718592 | tf_op jit(solution)/shard_map/contrast/pallas_call | solution.py:462
  219.4 2.0 results.1

commit v4 on v3

--- a/solution.py
+++ b/solution.py
@@ -21,9 +21,9 @@
 FAR_BIT = 8
 NEAR_BIT = 4
 CROSS_BITS = (5, 6, 7, 8)
-SUM_BITS = (0, 1, 2, 3, 4, 5, 6, 7, 8, 4, 0)
-ACROSS = len(SUM_BITS) - 2
-SUM_SLOTS = (2, 3, 4, 5, 7, 8, 9, 10, 11, 13, 14)
+SUM_BITS = (0, 4, 1, 2, 3, 5, 6, 7, 8, 4, 0)
+OVER, ACROSS = 1, len(SUM_BITS) - 2
+SUM_SLOTS = (2, 4, 5, 6, 7, 8, 9, 10, 11, 13, 14)
 FAR_SLOTS = (8, 12)
 LANES = 128
 TILES = D // LANES
@@ -200,16 +200,16 @@
         )
 
     def on_senders(step, act):
-        if step <= 4 or step > ACROSS:
+        if step < OVER or step > ACROSS:
             act()
         else:
-            pl.when(lower)(act)
+            pl.when(upper if step == OVER else lower)(act)
 
     def on_receivers(step, act):
-        if step == ACROSS:
-            pl.when(upper)(act)
+        if step < OVER or step > ACROSS:
+            act()
         else:
-            on_senders(step, act)
+            pl.when(upper if step == ACROSS else lower)(act)
 
     def block(src, dst, pair, k):
         rows = pl.ds(k * CHUNK, CHUNK)

time: 222 us -> 222 us (level)
  no operation moved by 1% of the time
where the time goes in v4:
time: 222 us
  Pallas kernels  220 us (99%)
    pallas_call x1, Pallas kernels, shards(): pl.pallas_call(kernel, name='contrast', out_shape=(wide, wide, jax.ShapeD...  217 us

profile of v4, /device:TPU:1, one launch (start us, length us, event | category | flops | bytes accessed | tf_op | source)
XLA Modules:
  0.0 221.6 jit_solution(1054530946914490353)
XLA Ops:
  1.9 217.5 %contrast.1 = (f32[256,1152]{1,0:T(8,128)S(1)}, f32[256,1152]{1,0:T(8,128)S(1)}, f32[2,11,1,128]{3,2,1,0:T(1,128)S(1)}) custom-call(f32[1]{0:T(128)} %bitcast.5.mult_hbm, f32[1]{0:T(128)} %bitcast.6.offs_hbm, f32[256,1152]{1,0:T(8,128)} %img_hbm.1, f32[256,1152]{1,0:T(8,128)} %txt_hbm.1, f32[1152]{0:T(1024)} %gi_hbm.1, f32[1152]{0:T(1024)} %gt_hbm.1), custom_call_target="tpu_custom_call" | custom-call | flops 1358954496 | bytes 4718592 | tf_op jit(solution)/shard_map/contrast/pallas_call | solution.py:462
  219.4 2.0 results.1
